TPU v7x, 32 devices: a whole 2x2x4 slice. The times are simulated.
32 devices in a mesh: guid: 2 (over x), req: 4 (over y, core), seq: 4 (over z).
Axes of the slice: x: 2, y: 2, z: 4, core: 2. Of those that a mesh axis runs over, the one named last changes fastest.
Arguments:
- img_hidden: bfloat16 [2, 24, 1024, 1536], P('guid', 'req', 'seq'), may hold values from -6 to 6
- txt_hidden: bfloat16 [2, 24, 192, 1536], P('guid', 'req', 'seq'), may hold values from -6 to 6
- img_mod: float32 [2, 24, 5, 1536], P('guid', 'req')
- txt_mod: float32 [2, 24, 2, 1536], P('guid', 'req'), may hold values from -3 to 3
- w_img_qkv: bfloat16 [1536, 3072], P(('guid', 'req', 'seq')), may hold values from -0.15625 to 0.15625
- w_txt_qkv: bfloat16 [1536, 3072], P(('guid', 'req', 'seq')), may hold values from -0.15625 to 0.15625
- w_out: bfloat16 [1024, 1536], P(('guid', 'req', 'seq')), may hold values from -0.1875 to 0.1875
- w_head: bfloat16 [1536, 64], P(('guid', 'req', 'seq')), may hold values from -0.15625 to 0.15625
- text_lengths: int32 [2, 24], P('guid', 'req'), may hold values from 1 to 154, as said below
- latent: float32 [24, 1024, 64], P('req', 'seq', 'guid'), may hold values from -6 to 6
- step: int32 [1], replicated, may hold values from 0 to 27
Outputs:
- advanced: float32 [24, 1024, 64], P('req', 'seq', 'guid')
- guided: float32 [24, 1024, 64], P('req', 'seq', 'guid')
Inputs may be any that keep to these rules, and one draw needn't show every extreme that they name: `text_lengths`: in each half one prompt has 154 text tokens and another has 1.
All inputs are finite; a program needn't handle non-finite values.
Results may differ from a plain program's by a relative error of at most 0.012.
The roundings to bfloat16 on the way count: a program that leaves them out, or rounds other values in their place, can miss the bound.
Values may be sent and summed in bfloat16 or wider, within the bound.
A program may use at most 256 MiB of HBM per device.

v0:
```python
import jax
import jax.numpy as jnp
from jax import lax
from jax.sharding import PartitionSpec as P

HD = 64
STEPS = 28


norm_epsilon = 1e-06
flow_shift = 3.0
guide_scale = 4.5


def partner(value, axis, bit):
    mask = 2**bit
    pairs = [(source, source ^ mask) for source in range(lax.axis_size(axis))]
    return lax.ppermute(value, axis, pairs)


def modulate(values_in, shift_vec, scale_vec):
    values_in = values_in.astype(jnp.float32)
    average = jnp.mean(values_in, axis=-1, keepdims=True)
    variance = jnp.mean((values_in - average) ** 2, axis=-1, keepdims=True)
    normed = (values_in - average) * lax.rsqrt(variance + norm_epsilon)
    return (normed * (1.0 + scale_vec[..., None, :]) + shift_vec[..., None, :]).astype(jnp.bfloat16)


def sigma_level(step_value):
    remaining = 1.0 - step_value / STEPS
    return flow_shift * remaining / (1.0 + (flow_shift - 1.0) * remaining)


def local(
    img_hidden,
    txt_hidden,
    img_mod,
    txt_mod,
    w_img_qkv,
    w_txt_qkv,
    w_out,
    w_head,
    text_lengths,
    latent,
    step,
):
    prompts = img_hidden.shape[1]
    img_rows = img_hidden.shape[2]
    txt_rows = txt_hidden.shape[2]
    dev_rows = img_rows + txt_rows
    model_width = img_hidden.shape[3]
    image_in = modulate(img_hidden[0], img_mod[0, :, 0], img_mod[0, :, 1])
    text_in = modulate(txt_hidden[0], txt_mod[0, :, 0], txt_mod[0, :, 1])
    full_img, full_txt, full_head = (
        lax.all_gather(w_img_qkv, ("guid", "req", "seq"), axis=0, tiled=True),
        lax.all_gather(w_txt_qkv, ("guid", "req", "seq"), axis=0, tiled=True),
        lax.all_gather(w_head, ("guid", "req", "seq"), axis=0, tiled=True),
    )
    attn_width = full_img.shape[1] // 3
    head_count = attn_width // HD
    qkv_image = jnp.einsum(
        "prd,de->pre", image_in, full_img, preferred_element_type=jnp.float32
    ).astype(jnp.bfloat16)
    qkv_text = jnp.einsum(
        "prd,de->pre", text_in, full_txt, preferred_element_type=jnp.float32
    ).astype(jnp.bfloat16)
    query_rows = qkv_image[..., :attn_width]
    key_rows = jnp.concatenate(
        [qkv_image[..., attn_width : 2 * attn_width], qkv_text[..., attn_width : 2 * attn_width]],
        axis=1,
    )
    value_rows = jnp.concatenate(
        [qkv_image[..., 2 * attn_width :], qkv_text[..., 2 * attn_width :]], axis=1
    )
    lengths = text_lengths[0]
    query_heads = query_rows.reshape(prompts, img_rows, head_count, HD)
    running = jnp.full((prompts, head_count, img_rows), -1e30, jnp.float32)
    key_piece = lax.all_gather(key_rows, "seq", axis=1, tiled=True)
    value_piece = lax.all_gather(value_rows, "seq", axis=1, tiled=True)
    piece_rows = key_piece.shape[1]
    key_heads = key_piece.reshape(prompts, piece_rows, head_count, HD)
    value_heads = value_piece.reshape(prompts, piece_rows, head_count, HD)
    scores = (
        jnp.einsum("pqhd,pkhd->phqk", query_heads, key_heads, preferred_element_type=jnp.float32)
        * 0.125
    )
    position = jnp.arange(piece_rows, dtype=jnp.int32)
    owner_dev = position // dev_rows
    offset = position % dev_rows
    text_pos = owner_dev * txt_rows + offset - img_rows
    allowed = (offset < img_rows)[None, :] | (text_pos[None, :] < lengths[:, None])
    scores = jnp.where(allowed[:, None, None, :], scores, -1e30)
    newest = jnp.maximum(running, jnp.max(scores, axis=-1))
    weights = jnp.exp(scores - newest[..., None])
    totals = jnp.sum(weights, axis=-1)
    accumulated = jnp.einsum(
        "phqk,pkhd->phqd",
        weights.astype(jnp.bfloat16),
        value_heads,
        preferred_element_type=jnp.float32,
    )
    running, totals, accumulated = (newest, totals, accumulated)
    mixture = accumulated / totals[..., None]
    attended = (
        jnp.transpose(mixture, (0, 2, 1, 3))
        .reshape(prompts, img_rows, attn_width)
        .astype(jnp.bfloat16)
    )
    flattened = attended.reshape(prompts * img_rows, attn_width)
    full_out = lax.all_gather(w_out, ("guid", "req", "seq"), axis=0, tiled=True)
    projected = jnp.dot(flattened, full_out, preferred_element_type=jnp.float32)
    residual = img_hidden[0].astype(jnp.float32) + img_mod[0, :, 2][:, None, :] * projected.reshape(
        prompts, img_rows, model_width
    )
    final_in = modulate(residual, img_mod[0, :, 3], img_mod[0, :, 4])
    guid_index = lax.axis_index("guid")
    half_width = latent.shape[2]
    own_start = guid_index * half_width
    other_start = (1 - guid_index) * half_width
    whole_velocity = jnp.einsum(
        "prd,dc->prc", final_in, full_head, preferred_element_type=jnp.float32
    )
    own_velocity = lax.dynamic_slice_in_dim(whole_velocity, own_start, half_width, 2)
    partner_part = lax.dynamic_slice_in_dim(whole_velocity, other_start, half_width, 2)
    other_velocity = partner(partner_part.astype(jnp.bfloat16), "guid", 0).astype(
        partner_part.dtype
    )
    cond_velocity = jnp.where(guid_index == 0, own_velocity, other_velocity)
    free_velocity = jnp.where(guid_index == 0, other_velocity, own_velocity)
    guided = free_velocity + guide_scale * (cond_velocity - free_velocity)
    step_value = step[0].astype(jnp.float32)
    advanced = latent + (sigma_level(step_value + 1.0) - sigma_level(step_value)) * guided
    return (advanced, guided)


def solution(mesh):
    placed = (
        P("guid", "req", "seq", None),
        P("guid", "req", "seq", None),
        P("guid", "req", None, None),
        P("guid", "req", None, None),
        P(("guid", "req", "seq"), None),
        P(("guid", "req", "seq"), None),
        P(("guid", "req", "seq"), None),
        P(("guid", "req", "seq"), None),
        P("guid", "req"),
        P("req", "seq", "guid"),
        P(),
    )
    return jax.shard_map(
        local,
        mesh=mesh,
        in_specs=placed,
        out_specs=(P("req", "seq", "guid"), P("req", "seq", "guid")),
        check_vma=False,
    )
```

profile of v0, /device:TPU:0, one launch (start us, length us, event | category | flops | bytes accessed | tf_op | source)
XLA Modules:
  0.0 797.2 jit_solution(6715840826499563582)
XLA Ops:
  7.2 0.7 all-gather.6.cloned.1.call-update
  8.0 0.7 all-gather.8.cloned.1.call-update
  8.7 1.5 convert_reduce_fusion.1
  10.2 1.7 fusion.36
  11.9 3.0 convert_reduce_fusion
  15.0 1.4 fusion.9
  16.6 79.1 %all-gather.6.cloned.1.call-done = bf16[1536,3072]{1,0:T(8,128)(2,1)} async-done(((bf16[48,3072]{1,0:T(8,128)(2,1)}), bf16[1536,3072]{1,0:T(8,128)(2,1)}) %all-gather.6.cloned.1.call-update) | async-done | bytes 9437200 | tf_op jit(solution)/shard_map/all_gather | solution.py:55
  95.7 19.2 %fusion.17 = bf16[6,256,3072]{2,1,0:T(8,128)(2,1)S(1)} fusion(bf16[1536,3072]{1,0:T(8,128)(2,1)} %all-gather.6.cloned.1.call-done, bf16[1,6,256,1536]{3,2,1,0:T(8,128)(2,1)} %param.11, f32[6,1536]{1,0:T(8,128)S(1)} %get-tuple-element.23, f32[6,1536]{1,0:T(8,128)S(1)} %get-tuple-element.22, f32[6,256]{1,0:T(8,128)S(1)} %add_rsqrt_fusion.1, ...), kind=kOutput, calls=%fused_computation.22 | convolution fusion | flops 14514388992 | bytes 23678976 | tf_op jit(solution)/shard_map/prd,de->pre/dot_general | solution.py:61
  114.9 3.3 fusion.62
  118.1 61.1 %all-gather.8.cloned.1.call-done = bf16[1536,3072]{1,0:T(8,128)(2,1)} async-done(((bf16[48,3072]{1,0:T(8,128)(2,1)}), bf16[1536,3072]{1,0:T(8,128)(2,1)}) %all-gather.8.cloned.1.call-update) | async-done | bytes 9437200 | tf_op jit(solution)/shard_map/all_gather | solution.py:56
  179.3 7.2 fusion.27
  186.4 0.9 fusion.63
  187.4 2.6 pad_maximum_fusion.1
  190.0 3.4 pad_maximum_fusion
  193.5 0.5 all-gather.14.cloned.1.call-update
  194.0 0.6 copy.48
  194.7 108.6 %all_gather.23 = bf16[1536,64]{1,0:T(8,128)(2,1)} all-gather(bf16[48,64]{1,0:T(8,128)(2,1)S(1)} %copy-done.9), channel_id=1, replica_groups=mesh['guid'=2,'req'=4,'seq'=4] {'guid','req','seq'}, dimensions={0}, use_global_device_ids=true | all-gather | bytes 202752 | tf_op jit(solution)/shard_map/all_gather | solution.py:57
  303.2 0.6 fusion.49
  304.0 3.2 copy.20
  307.2 145.5 %all-gather.10.cloned.1.call-done = bf16[6,1216,1024]{2,1,0:T(8,128)(2,1)} async-done(((bf16[6,304,1024]{2,1,0:T(8,128)(2,1)}), bf16[6,1216,1024]{2,1,0:T(8,128)(2,1)}) %all-gather.10.cloned.1.call-update) | async-done | bytes 14942224 | tf_op jit(solution)/shard_map/all_gather | solution.py:78
  452.7 19.9 %copy.23 = bf16[6,1216,1024]{1,2,0:T(8,128)(2,1)} copy(bf16[6,1216,1024]{2,1,0:T(8,128)(2,1)} %all-gather.10.cloned.1.call-done) | data formatting | bytes 29884416 | tf_op jit(solution)/shard_map/all_gather | solution.py:78
  472.6 49.5 %fusion.66 = (f32[6,16,256]{2,1,0:T(8,128)S(1)}, f32[6,16,256,1216]{2,3,1,0:T(8,128)}) fusion(bf16[6,256,16,64]{1,3,2,0:T(8,128)(2,1)S(1)} %bitcast.86, bf16[6,1216,16,64]{1,3,2,0:T(8,128)(2,1)} %bitcast.84, pred[6,1216]{1,0:T(8,128)(4,1)S(1)} %compare_or_fusion), kind=kOutput, calls=%fused_computation.91 | convolution fusion | flops 3914833920 | bytes 137731200 | tf_op jit(solution)/shard_map/pqhd,pkhd->phqk/dot_general | solution.py:84
  522.1 36.5 %fusion = f32[6,16,256]{2,1,0:T(8,128)S(1)} fusion(f32[6,16,256,1216]{2,3,1,0:T(8,128)} %get-tuple-element.17, f32[6,16,256]{2,1,0:T(8,128)S(1)} %broadcast_maximum_fusion), kind=kLoop, calls=%fused_computation.2 | loop fusion | flops 59744256 | bytes 119734272 | tf_op jit(solution)/shard_map/reduce_sum | solution.py:95
  558.6 150.6 %all-gather.12.cloned.1.call-done = bf16[6,1216,1024]{2,1,0:T(8,128)(2,1)} async-done(((bf16[6,304,1024]{2,1,0:T(8,128)(2,1)}), bf16[6,1216,1024]{2,1,0:T(8,128)(2,1)}) %all-gather.12.cloned.1.call-update) | async-done | bytes 14942224 | tf_op jit(solution)/shard_map/all_gather | solution.py:79
  709.3 19.1 %copy.24 = bf16[6,1216,1024]{1,2,0:T(8,128)(2,1)} copy(bf16[6,1216,1024]{2,1,0:T(8,128)(2,1)} %all-gather.12.cloned.1.call-done) | data formatting | bytes 29884416 | tf_op jit(solution)/shard_map/all_gather | solution.py:79
  728.4 44.2 %fusion.20 = bf16[6,256,16,64]{1,3,2,0:T(8,128)(2,1)S(1)} fusion(f32[6,256,16]{1,2,0:T(8,128)S(1)} %bitcast.88, bf16[6,1216,16,64]{1,3,2,0:T(8,128)(2,1)} %bitcast.85, f32[6,16,256,1216]{2,3,1,0:T(8,128)} %get-tuple-element.17, f32[6,16,256]{2,1,0:T(8,128)S(1)} %broadcast_maximum_fusion), kind=kOutput, calls=%fused_computation.24 | convolution fusion | flops 3888119808 | bytes 137822208 | tf_op jit(solution)/shard_map/phqk,pkhd->phqd/dot_general | solution.py:96
  772.7 8.7 %fusion.67 = (f32[6,256]{1,0:T(8,128)S(1)}, f32[6,256,1536]{2,1,0:T(8,128)S(1)}) fusion(bf16[6,256,1024]{1,2,0:T(8,128)(2,1)S(1)} %bitcast.87, bf16[1024,1536]{1,0:T(8,128)(2,1)} %all-gather.14.cloned.1.call-done, f32[6,1536]{1,0:T(8,128)S(1)} %bitcast.89, bf16[1,6,256,1536]{3,2,1,0:T(8,128)(2,1)} %param.11), kind=kOutput, calls=%fused_computation.92 | convolution fusion | flops 4841273856 | bytes 20490240 | tf_op jit(solution)/shard_map/dot_general | solution.py:111
  781.5 1.1 multiply_reduce_fusion
  782.6 2.3 fusion.26
  785.0 1.5 collective-permute-start
  787.2 2.6 collective-permute-done
  789.8 0.8 multiply_add_fusion
  (45 shorter events, 0.6 us)
Async XLA Ops:
  7.2 9.2 %copy-start.5 = (f32[1,6,2,1536]{3,2,1,0:T(2,128)S(1)}, f32[1,6,2,1536]{3,2,1,0:T(2,128)}, u32[]{:S(2)}) copy-start(f32[1,6,2,1536]{3,2,1,0:T(2,128)} %param.14) | copy-start | bytes 221188
  7.2 9.3 %copy-start.4 = (f32[1,6,5,1536]{3,0,2,1:T(1,128)S(1)}, f32[1,6,5,1536]{3,0,2,1:T(1,128)}, u32[]{:S(2)}) copy-start(f32[1,6,5,1536]{3,0,2,1:T(1,128)} %param.13) | copy-start | bytes 552964
  7.2 88.5 %all-gather.6.cloned.1.call-start = ((), (), s32[]{:S(2)}) async-start(), calls=%async_computation | async-start | bytes 9732096 | tf_op jit(solution)/shard_map/all_gather | solution.py:55
  7.9 171.3 %all-gather.8.cloned.1.call-start = ((), (), s32[]{:S(2)}) async-start(), calls=%async_computation.1 | async-start | bytes 9732096 | tf_op jit(solution)/shard_map/all_gather | solution.py:56
  8.7 444.0 %all-gather.10.cloned.1.call-start = ((), (), s32[]{:S(2)}) async-start(), calls=%async_computation.2 | async-start | bytes 18677760 | tf_op jit(solution)/shard_map/all_gather | solution.py:78
  8.7 6.3 copy-start
  179.3 8.1 %copy-start.1 = (bf16[6,256,1024]{2,1,0:T(8,128)(2,1)S(1)}, bf16[6,256,1024]{2,1,0:T(8,128)(2,1)}, u32[]{:S(2)}) copy-start(bf16[6,256,1024]{2,1,0:T(8,128)(2,1)} %get-tuple-element.5) | copy-start | bytes 9437188
  190.0 4.7 copy-start.9
  190.0 113.9 %copy-start.10 = (s32[1,6]{1,0:T(1,128)S(1)}, s32[1,6]{1,0:T(1,128)}, u32[]{:S(2)}) copy-start(s32[1,6]{1,0:T(1,128)} %param.19) | copy-start | bytes 76
  190.0 519.3 %all-gather.12.cloned.1.call-start = ((), (), s32[]{:S(2)}) async-start(), calls=%async_computation.3 | async-start | bytes 18677760 | tf_op jit(solution)/shard_map/all_gather | solution.py:79
  193.4 579.3 %all-gather.14.cloned.1.call-start = ((), (), s32[]{:S(2)}) async-start(), calls=%async_computation.4 | async-start | bytes 3244032 | tf_op jit(solution)/shard_map/all_gather | solution.py:110
  728.4 44.3 %copy-start.6 = (f32[1,6,1,1536]{3,1,2,0:T(8,128)S(1)}, f32[1,6,1,1536]{3,1,2,0:T(8,128)}, u32[]{:S(2)}) copy-start(f32[1,6,1,1536]{3,1,2,0:T(8,128)} %copy.48) | copy-start | bytes 110596
  781.4 1.1 copy-start.2
  781.4 1.1 copy-start.7
  781.4 1.1 copy-start.8
  781.4 8.4 %copy-start.3 = (f32[6,256,32]{1,2,0:T(8,128)S(1)}, f32[6,256,32]{1,2,0:T(8,128)}, u32[]{:S(2)}) copy-start(f32[6,256,32]{1,2,0:T(8,128)} %param.20) | copy-start | bytes 589828
  785.0 4.9 collective-permute-start
Sparse Core Ops, SparseCore 0:
  10.9 84.7 all-gather.5
  98.6 80.6 all-gather.7
  190.1 262.5 all-gather.9
  454.1 255.1 all-gather.11
  712.0 57.2 all-gather.13
where the time goes:
time: 798 us; the launch traced here: 797 us
  waiting for transfers between devices  441 us (55%)
  matrix products  131 us (16%)
  blocking collectives  109 us (14%)
  other arithmetic  52.8 us (7%)
  local copies, waits for them, and re-layouts  47.2 us (6%)
  between operations  14.8 us (2%)
    all_gather x1, waiting for transfers between devices, local(): value_piece = lax.all_gather(value_rows, 'seq', axis=1, tiled=True)  151 us
    all_gather x1, waiting for transfers between devices, local(): key_piece = lax.all_gather(key_rows, 'seq', axis=1, tiled=True)  146 us
    all_gather x1, blocking collectives, local(): lax.all_gather(w_head, ('guid', 'req', 'seq'), axis=0, tiled=True)  109 us
    all_gather x1, waiting for transfers between devices, local(): lax.all_gather(w_img_qkv, ('guid', 'req', 'seq'), axis=0, tiled=True)  79.1 us
    all_gather x1, waiting for transfers between devices, local(): lax.all_gather(w_txt_qkv, ('guid', 'req', 'seq'), axis=0, tiled=True)  61.1 us
    dot_general x1, matrix products, local(): jnp.einsum('pqhd,pkhd->phqk', query_heads, key_heads, preferred_element_t...  49.5 us
    dot_general x1, matrix products, local(): jnp.einsum('phqk,pkhd->phqd', weights.astype(jnp.bfloat16), value_heads,...  44.2 us
    reduce_sum x1, other arithmetic, local(): totals = jnp.sum(weights, axis=-1)  36.5 us
  transfers between devices with their start and end apart: 6, of which 5 were waited for; matrix products, arithmetic and copies ran while one was open for 26% of the time, Pallas kernels for 0%

commit v1 on v0

--- a/solution.py
+++ b/solution.py
@@ -1,6 +1,10 @@
+import functools
+
 import jax
 import jax.numpy as jnp
 from jax import lax
+from jax.experimental import pallas as pl
+from jax.experimental.pallas import tpu as pltpu
 from jax.sharding import PartitionSpec as P
 
 HD = 64
@@ -133,6 +137,220 @@
     return (advanced, guided)
 
 
+ALL_AXES = ("guid", "req", "seq")
+LOG2E = 1.4426950408889634
+
+
+def attend_kernel(images, texts, *refs):
+    q_ref, o_ref = refs[0], refs[-1]
+    pieces = []
+    at = 1
+    for _ in range(images):
+        pieces.append((refs[at], refs[at + 1], None))
+        at += 2
+    for _ in range(texts):
+        pieces.append((refs[at], refs[at + 1], refs[at + 2]))
+        at += 3
+    q = q_ref[...] * jnp.asarray(0.125, jnp.bfloat16)
+    lane = lax.broadcasted_iota(jnp.int32, q.shape, 1)
+    halves = []
+    for head in range(2):
+        mine = (lane < HD) if head == 0 else (lane >= HD)
+        q_head = jnp.where(mine, q, jnp.zeros_like(q))
+        scores = []
+        for k_ref, _, bias_ref in pieces:
+            s = lax.dot_general(
+                q_head, k_ref[...], (((1,), (1,)), ((), ())), preferred_element_type=jnp.float32
+            )
+            if bias_ref is not None:
+                s = s + bias_ref[0:1, :]
+            scores.append(s)
+        top = functools.reduce(jnp.maximum, [jnp.max(s, axis=1, keepdims=True) for s in scores])
+        top = top * LOG2E
+        total = None
+        mixed = None
+        for s, (_, v_ref, _) in zip(scores, pieces):
+            p = jnp.exp2(s * LOG2E - top)
+            part = jnp.sum(p, axis=1, keepdims=True)
+            total = part if total is None else total + part
+            part = jnp.dot(p.astype(jnp.bfloat16), v_ref[...], preferred_element_type=jnp.float32)
+            mixed = part if mixed is None else mixed + part
+        halves.append(mixed / total)
+    o_ref[...] = jnp.where(lane < HD, halves[0], halves[1]).astype(jnp.bfloat16)
+
+
+def attend(query, width, images, texts):
+    rows = query.shape[0]
+    block = min(256, rows)
+    pairs = width // 128
+    args = [query]
+    specs = [pl.BlockSpec((block, 128), lambda h, i: (i, h))]
+
+    def column(array, start):
+        args.append(array)
+        specs.append(pl.BlockSpec((array.shape[0], 128), lambda h, i: (0, start // 128 + h)))
+
+    keys = 0
+    for array, key_at, value_at in images:
+        column(array, key_at)
+        column(array, value_at)
+        keys += array.shape[0]
+    for array, key_at, value_at, bias in texts:
+        column(array, key_at)
+        column(array, value_at)
+        args.append(bias)
+        specs.append(pl.BlockSpec(bias.shape, lambda h, i: (0, 0)))
+        keys += array.shape[0]
+    return pl.pallas_call(
+        functools.partial(attend_kernel, len(images), len(texts)),
+        grid=(pairs, rows // block),
+        in_specs=specs,
+        out_specs=pl.BlockSpec((block, 128), lambda h, i: (i, h)),
+        out_shape=jax.ShapeDtypeStruct((rows, width), jnp.bfloat16),
+        compiler_params=pltpu.CompilerParams(vmem_limit_bytes=28 * 2**20),
+        cost_estimate=pl.CostEstimate(
+            flops=16 * rows * keys * width,
+            bytes_accessed=4 * (rows + keys) * width,
+            transcendentals=rows * keys * width // HD,
+        ),
+    )(*args)
+
+
+def text_bias(position, length):
+    bias = jnp.where(position < length, 0.0, -1e30).astype(jnp.float32)
+    return jnp.broadcast_to(bias[None, :], (8, bias.shape[0]))
+
+
+def moved(
+    img_hidden,
+    txt_hidden,
+    img_mod,
+    txt_mod,
+    w_img_qkv,
+    w_txt_qkv,
+    w_out,
+    w_head,
+    text_lengths,
+    latent,
+    step,
+):
+    ranks = lax.axis_size("seq")
+    seq = lax.axis_index("seq")
+    core = lax.axis_index("req") % 2
+    guid = lax.axis_index("guid")
+    attn_width = w_out.shape[0] * lax.axis_size(ALL_AXES)
+    model_width = img_hidden.shape[3]
+    img_rows, txt_rows = img_hidden.shape[2], txt_hidden.shape[2]
+    img_half, txt_half = img_rows // 2, txt_rows // 2
+
+    def swap(value):
+        count = lax.axis_size("req")
+        return lax.ppermute(value, "req", [(r, r ^ 1) for r in range(count)])
+
+    def hop(value, k):
+        return lax.ppermute(value, "seq", [(r, r ^ k) for r in range(ranks)])
+
+    def pick(value, index):
+        return lax.dynamic_index_in_dim(value, index, 0, keepdims=False)
+
+    def spread(value):
+        return [pick(value, seq)] + [hop(pick(value, seq ^ k), k) for k in range(1, ranks)]
+
+    def by_core(mine, other, axis):
+        return jnp.where(
+            core == 0,
+            jnp.concatenate([mine, other], axis),
+            jnp.concatenate([other, mine], axis),
+        )
+
+    def halved(value, rows):
+        kept = lax.dynamic_slice_in_dim(value, core * rows, rows, 1)
+        sent = lax.dynamic_slice_in_dim(value, (1 - core) * rows, rows, 1)
+        return by_core(kept, swap(sent), 0)
+
+    full_img = lax.all_gather(w_img_qkv, ALL_AXES, axis=0, tiled=True)
+    full_txt = lax.all_gather(w_txt_qkv[:, attn_width:], ALL_AXES, axis=0, tiled=True)
+    head_lines = w_head.size // model_width
+    tail = jnp.concatenate([w_out, w_head.reshape(head_lines, model_width)], 0)
+    full_tail = lax.all_gather(tail, ALL_AXES, axis=0, tiled=False)
+    full_out = full_tail[:, : w_out.shape[0]].reshape(attn_width, model_width)
+    full_head = full_tail[:, w_out.shape[0] :].reshape(model_width, w_head.shape[1])
+
+    img_own = jnp.concatenate(spread(img_hidden[0, :ranks]), 0)
+    txt_own = jnp.concatenate(spread(txt_hidden[0, :ranks]), 0)
+    img_pair = jnp.concatenate(spread(halved(img_hidden[0, ranks:], img_half)), 0)
+    txt_pair = jnp.concatenate(spread(halved(txt_hidden[0, ranks:], txt_half)), 0)
+    mod_own, tmod_own, len_own = pick(img_mod[0], seq), pick(txt_mod[0], seq), pick(text_lengths[0], seq)
+    mod_pair = pick(by_core(img_mod[0, ranks:], swap(img_mod[0, ranks:]), 0), seq)
+    tmod_pair = pick(by_core(txt_mod[0, ranks:], swap(txt_mod[0, ranks:]), 0), seq)
+    len_pair = pick(by_core(text_lengths[0, ranks:], swap(text_lengths[0, ranks:]), 0), seq)
+
+    def dot(left, right):
+        return jnp.dot(left, right, preferred_element_type=jnp.float32)
+
+    def places(start, count):
+        slots = jnp.arange(ranks, dtype=jnp.int32) ^ seq
+        return (slots[:, None] * txt_rows + start + jnp.arange(count, dtype=jnp.int32)[None]).reshape(-1)
+
+    qkv_own = dot(modulate(img_own, mod_own[0], mod_own[1]), full_img).astype(jnp.bfloat16)
+    kvt_own = dot(modulate(txt_own, tmod_own[0], tmod_own[1]), full_txt).astype(jnp.bfloat16)
+    qkv_pair = dot(modulate(img_pair, mod_pair[0], mod_pair[1]), full_img).astype(jnp.bfloat16)
+    kvt_pair = dot(modulate(txt_pair, tmod_pair[0], tmod_pair[1]), full_txt).astype(jnp.bfloat16)
+    kv_other = swap(qkv_pair[:, attn_width:])
+    kvt_other = swap(kvt_pair)
+
+    attended_own = attend(
+        qkv_own,
+        attn_width,
+        [(qkv_own, attn_width, 2 * attn_width)],
+        [(kvt_own, 0, attn_width, text_bias(places(0, txt_rows), len_own))],
+    )
+    attended_pair = attend(
+        qkv_pair,
+        attn_width,
+        [(qkv_pair, attn_width, 2 * attn_width), (kv_other, 0, attn_width)],
+        [
+            (kvt_pair, 0, attn_width, text_bias(places(core * txt_half, txt_half), len_pair)),
+            (kvt_other, 0, attn_width, text_bias(places((1 - core) * txt_half, txt_half), len_pair)),
+        ],
+    )
+
+    def finish(attended, hidden, mod):
+        residual = hidden.astype(jnp.float32) + mod[2] * dot(attended, full_out)
+        return dot(modulate(residual, mod[3], mod[4]), full_head)
+
+    velocity = jnp.concatenate(
+        [
+            finish(attended_own, img_own, mod_own).reshape(ranks, img_rows, -1),
+            finish(attended_pair, img_pair, mod_pair).reshape(ranks, img_half, -1),
+        ],
+        1,
+    )
+    part = latent.shape[2]
+    own = lax.dynamic_slice_in_dim(velocity, guid * part, part, 2)
+    sent = lax.dynamic_slice_in_dim(velocity, (1 - guid) * part, part, 2).astype(jnp.bfloat16)
+    other = partner(sent, "guid", 0).astype(jnp.float32)
+    cond = jnp.where(guid == 0, own, other)
+    free = jnp.where(guid == 0, other, own)
+    guided = free + guide_scale * (cond - free)
+    back = jnp.stack([guided[0]] + [hop(guided[k], k) for k in range(1, ranks)])
+    back = jnp.stack([pick(back, seq ^ p) for p in range(ranks)])
+    shared = back[:, img_rows:]
+    kept = lax.dynamic_slice_in_dim(shared, core * (ranks // 2), ranks // 2, 0)
+    given = lax.dynamic_slice_in_dim(shared, (1 - core) * (ranks // 2), ranks // 2, 0)
+    guided = jnp.concatenate([back[:, :img_rows], by_core(kept, swap(given), 1)], 0)
+    step_value = step[0].astype(jnp.float32)
+    advanced = latent + (sigma_level(step_value + 1.0) - sigma_level(step_value)) * guided
+    return (advanced, guided)
+
+
+def block(img_hidden, *others):
+    ranks = lax.axis_size("seq")
+    if ranks & (ranks - 1) == 0 and 2 * img_hidden.shape[1] == 3 * ranks and lax.axis_size("req") % 2 == 0:
+        return moved(img_hidden, *others)
+    return local(img_hidden, *others)
+
+
 def solution(mesh):
     placed = (
         P("guid", "req", "seq", None),
@@ -148,7 +366,7 @@
         P(),
     )
     return jax.shard_map(
-        local,
+        block,
         mesh=mesh,
         in_specs=placed,
         out_specs=(P("req", "seq", "guid"), P("req", "seq", "guid")),

time: 798 us -> 421 us (0.53)
  waiting for transfers between devices: 441 us -> 183 us
  blocking collectives: 109 us -> 0 us
  matrix products: 131 us -> 34.8 us
  Pallas kernels: 0 us -> 73.1 us
  starting transfers between devices: 1.74 us -> 68.6 us
  other arithmetic: 52.8 us -> 22 us
  local copies, waits for them, and re-layouts: 47.2 us -> 23.4 us
    all_gather x5 -> x3, waiting for transfers between devices: 436 us -> 97.5 us  [the longest x1 77.3 us: moved(): full_img = lax.all_gather(w_img_qkv, ALL_AXES, axis=0, tiled=True)]
    all_gather x1 -> x0, blocking collectives: 109 us -> none  [local(): lax.all_gather(w_head, ('guid', 'req', 'seq'), axis=0, tiled=True)]
    dot_general x6 -> x8, matrix products: 131 us -> 34.8 us  [dot(): return jnp.dot(left, right, preferred_element_type=jnp.float32)]
    ppermute x0 -> x23, waiting for transfers between devices: none -> 81.5 us  [the longest x15 80.3 us: hop(): return lax.ppermute(value, 'seq', [(r, r ^ k) for r in range(ranks)])]
    pallas_call x0 -> x2, Pallas kernels: none -> 73.1 us  [attend(): pl.pallas_call(functools.partial(attend_kernel, len(images), len(texts)),...]
    ppermute x0 -> x23, starting transfers between devices: none -> 67 us  [the longest x15 65.3 us: hop(): return lax.ppermute(value, 'seq', [(r, r ^ k) for r in range(ranks)])]
    all_gather x2 -> x0, local copies, waits for them, and re-layouts: 39 us -> none  [the longest x1 19.9 us: local(): key_piece = lax.all_gather(key_rows, 'seq', axis=1, tiled=True)]
    reduce_sum x1 -> x0, other arithmetic: 36.5 us -> none  [local(): totals = jnp.sum(weights, axis=-1)]
  transfers between devices with their start and end apart: 6 -> 27, of which waited for: 5 -> 11; matrix products, arithmetic and copies ran while one was open for 26% -> 17% of each run, Pallas kernels for 0% -> 11%
where the time goes in v1:
time: 421 us; the launch traced here: 420 us
  waiting for transfers between devices  183 us (43%)
  Pallas kernels  73.1 us (17%)
  starting transfers between devices  68.6 us (16%)
  matrix products  34.8 us (8%)
  local copies, waits for them, and re-layouts  23.4 us (6%)
  other arithmetic  22 us (5%)
  between operations  15.2 us (4%)
    ppermute x15, waiting for transfers between devices, hop(): return lax.ppermute(value, 'seq', [(r, r ^ k) for r in range(ranks)])  80.3 us
    all_gather x1, waiting for transfers between devices, moved(): full_img = lax.all_gather(w_img_qkv, ALL_AXES, axis=0, tiled=True)  77.3 us
    pallas_call x2, Pallas kernels, attend(): pl.pallas_call(functools.partial(attend_kernel, len(images), len(texts)),...  73.1 us
    ppermute x15, starting transfers between devices, hop(): return lax.ppermute(value, 'seq', [(r, r ^ k) for r in range(ranks)])  65.3 us
    dot_general x8, matrix products, dot(): return jnp.dot(left, right, preferred_element_type=jnp.float32)  34.8 us
    all_gather x1, waiting for transfers between devices, moved(): lax.all_gather(w_txt_qkv[:, attn_width:], ALL_AXES, axis=0, tiled=True)  20.2 us
  transfers between devices with their start and end apart: 27, of which 11 were waited for; matrix products, arithmetic and copies ran while one was open for 17% of the time, Pallas kernels for 11%

profile of v1, /device:TPU:0, one launch (start us, length us, event | category | flops | bytes accessed | tf_op | source)
XLA Modules:
  0.0 420.4 jit_solution(17133723733865679878)
XLA Ops:
  8.1 1.6 maximum_bitcast_fusion
  9.7 1.6 slice.117
  18.6 5.0 %collective-permute-start.5 = (bf16[48,1536]{1,0:T(8,128)(2,1)}, bf16[48,1536]{1,0:T(8,128)(2,1)S(1)}, u32[]{:S(2)}, u32[]{:S(2)}) collective-permute-start(bf16[48,1536]{1,0:T(8,128)(2,1)} %get-tuple-element.29), channel_id=1, source_target_pairs={{0,3},{1,2},{2,1},{3,0},{4,7},{5,6},{6,5},{7,4},{8,11},{9,10},{10,... | collective-permute-start | bytes 442376 | tf_op jit(solution)/shard_map/ppermute | solution.py:251
  26.2 1.5 fusion.71
  30.2 1.5 dynamic-slice_bitcast_fusion.5
  38.6 3.8 collective-permute-start.2
  44.2 3.8 collective-permute-start.13
  49.1 16.4 %collective-permute-done.15 = bf16[24,1536]{1,0:T(8,128)(2,1)S(1)} collective-permute-done((bf16[24,1536]{1,0:T(8,128)(2,1)S(1)}, bf16[24,1536]{1,0:T(8,128)(2,1)S(1)}, u32[]{:S(2)}, u32[]{:S(2)}) %collective-permute-start.15) | collective-permute-done | bytes 73760 | tf_op jit(solution)/shard_map/ppermute | solution.py:251
  65.5 29.9 %collective-permute-start.1 = (bf16[256,1536]{1,0:T(8,128)(2,1)}, bf16[256,1536]{1,0:T(8,128)(2,1)S(1)}, u32[]{:S(2)}, u32[]{:S(2)}) collective-permute-start(bf16[256,1536]{1,0:T(8,128)(2,1)} %get-tuple-element.20), channel_id=1, source_target_pairs={{0,2},{1,3},{2,0},{3,1},{4,6},{5,7},{6,4},{7,5},{8,10},{9,11},{10,... | collective-permute-start | bytes 2359304 | tf_op jit(solution)/shard_map/ppermute | solution.py:251
  95.4 5.7 %collective-permute-done.14 = bf16[24,1536]{1,0:T(8,128)(2,1)S(1)} collective-permute-done((bf16[24,1536]{1,0:T(8,128)(2,1)S(1)}, bf16[24,1536]{1,0:T(8,128)(2,1)S(1)}, u32[]{:S(2)}, u32[]{:S(2)}) %collective-permute-start.14) | collective-permute-done | bytes 73760 | tf_op jit(solution)/shard_map/ppermute | solution.py:251
  101.2 11.8 %collective-permute-start = (bf16[256,1536]{1,0:T(8,128)(2,1)}, bf16[256,1536]{1,0:T(8,128)(2,1)S(1)}, u32[]{:S(2)}, u32[]{:S(2)}) collective-permute-start(bf16[256,1536]{1,0:T(8,128)(2,1)} %get-tuple-element.21), channel_id=1, source_target_pairs={{0,1},{1,0},{2,3},{3,2},{4,5},{5,4},{6,7},{7,6},{8,9},{9,8},{10,11... | collective-permute-start | bytes 2359304 | tf_op jit(solution)/shard_map/ppermute | solution.py:251
  113.7 4.1 collective-permute-start.9
  119.0 31.8 %collective-permute-done.1 = bf16[256,1536]{1,0:T(8,128)(2,1)S(1)} collective-permute-done((bf16[256,1536]{1,0:T(8,128)(2,1)}, bf16[256,1536]{1,0:T(8,128)(2,1)S(1)}, u32[]{:S(2)}, u32[]{:S(2)}) %collective-permute-start.1) | collective-permute-done | bytes 786464 | tf_op jit(solution)/shard_map/ppermute | solution.py:251
  150.9 1.9 collective-permute-done
  153.3 2.9 fusion.2
  156.9 21.9 %collective-permute-done.8 = bf16[128,1536]{1,0:T(8,128)(2,1)S(1)} collective-permute-done((bf16[128,1536]{1,0:T(8,128)(2,1)S(1)}, bf16[128,1536]{1,0:T(8,128)(2,1)S(1)}, u32[]{:S(2)}, u32[]{:S(2)}) %collective-permute-start.8) | collective-permute-done | bytes 393248 | tf_op jit(solution)/shard_map/ppermute | solution.py:251
  182.3 4.7 %slice.141 = bf16[32,32,1536]{2,1,0:T(8,128)(2,1)} slice(bf16[32,34,1536]{2,1,0:T(8,128)(2,1)} %all-gather.10.cloned.1.call-done), slice={[0:32], [0:32], [0:1536]} | slice | bytes 6291456 | tf_op jit(solution)/shard_map/slice | solution.py:276
  187.0 20.2 %all-gather.8.cloned.1.call-done = bf16[1536,2048]{1,0:T(8,128)(2,1)} async-done(((bf16[48,2048]{1,0:T(8,128)(2,1)}), bf16[1536,2048]{1,0:T(8,128)(2,1)}) %all-gather.8.cloned.1.call-update) | async-done | bytes 6291472 | tf_op jit(solution)/shard_map/all_gather | solution.py:272
  207.3 4.1 convolution_convert_fusion.3.refs_5_.refs_6_
  211.9 1.5 convolution_convert_fusion.2.refs_3_.refs_4_
  213.4 77.3 %all-gather.6.cloned.1.call-done = bf16[1536,3072]{1,0:T(8,128)(2,1)} async-done(((bf16[48,3072]{1,0:T(8,128)(2,1)}), bf16[1536,3072]{1,0:T(8,128)(2,1)}) %all-gather.6.cloned.1.call-update) | async-done | bytes 9437200 | tf_op jit(solution)/shard_map/all_gather | solution.py:271
  290.7 9.1 %convolution_convert_fusion.1.refs_0_.refs_1_.refs_2_ = bf16[512,3072]{1,0:T(8,128)(2,1)S(1)} fusion(bf16[1536,3072]{1,0:T(8,128)(2,1)} %all-gather.6.cloned.1.call-done, f32[1536]{0:T(1024)} %get-tuple-element.10, f32[1536]{0:T(1024)} %get-tuple-element.11, f32[512]{0:T(512)} %add_rsqrt_fusion.3, f32[512]{0:T(512)} %copy-done.29, ...), kind=kOutput, calls=%fused_computation.15 | convolution fusion | flops 4843634688 | bytes 14172160 | tf_op jit(solution)/shard_map/dot_general | solution.py:289
  302.2 12.9 %convolution_convert_fusion.refs_0_.refs_1_.refs_2_ = bf16[1024,3072]{1,0:T(8,128)(2,1)S(1)} fusion(bf16[1536,3072]{1,0:T(8,128)(2,1)} %all-gather.6.cloned.1.call-done, f32[1536]{0:T(1024)S(1)} %copy-done.31, f32[1536]{0:T(1024)S(1)} %copy-done.32, f32[1024]{0:T(1024)S(1)} %copy-done.39, f32[1024]{0:T(1024)S(1)} %copy-done.28, ...), kind=kOutput, calls=%fused_computation.11 | convolution fusion | flops 9687269376 | bytes 18894848 | tf_op jit(solution)/shard_map/dot_general | solution.py:289
  315.1 47.1 %shard_map.122 = bf16[1024,1024]{1,0:T(8,128)(2,1)S(1)} custom-call(bf16[1024,3072]{1,0:T(8,128)(2,1)S(1)} %convolution_convert_fusion.refs_0_.refs_1_.refs_2_, bf16[1024,3072]{1,0:T(8,128)(2,1)S(1)} %convolution_convert_fusion.refs_0_.refs_1_.refs_2_, bf16[1024,3072]{1,0:T(8,128)(2,1)S(1)} %convolution_convert_fusion.refs_0_.refs_1_.refs_2_, ...), custom_call_target="tpu_custom_call" | custom-call | flops 20401094656 | bytes 9175040 | tf_op jit(solution)/shard_map/pallas_call | solution.py:204
  362.2 3.6 fusion.82
  369.2 26.0 %shard_map.123 = bf16[512,1024]{1,0:T(8,128)(2,1)S(1)} custom-call(bf16[512,3072]{1,0:T(8,128)(2,1)S(1)} %convolution_convert_fusion.1.refs_0_.refs_1_.refs_2_, bf16[512,3072]{1,0:T(8,128)(2,1)S(1)} %convolution_convert_fusion.1.refs_0_.refs_1_.refs_2_, bf16[512,3072]{1,0:T(8,128)(2,1)S(1)} %convolution_convert_fusion.1.refs_0_.refs_1_.refs_2_, ...), custom_call_target="tpu_custom_call" | custom-call | flops 10200547328 | bytes 7077888 | tf_op jit(solution)/shard_map/pallas_call | solution.py:204
  395.3 1.9 fusion.83
  398.9 1.5 collective-permute-start.19
  400.4 3.5 collective-permute-done.19
  404.0 2.0 collective-permute-start.22
  407.0 1.5 collective-permute-start.20
  410.2 1.5 collective-permute-done.21
  (204 shorter events, 41.4 us)
Async XLA Ops:
  7.2 173.5 %all-gather.10.cloned.1.call-start = ((), (), s32[]{:S(2)}) async-start(), calls=%async_computation.2 | async-start | bytes 4055040 | tf_op jit(solution)/shard_map/all_gather | solution.py:275
  9.6 197.6 %all-gather.8.cloned.1.call-start = ((), (), s32[]{:S(2)}) async-start(), calls=%async_computation.1 | async-start | bytes 6488064 | tf_op jit(solution)/shard_map/all_gather | solution.py:272
  11.3 279.3 %all-gather.6.cloned.1.call-start = ((), (), s32[]{:S(2)}) async-start(), calls=%async_computation | async-start | bytes 9732096 | tf_op jit(solution)/shard_map/all_gather | solution.py:271
  12.8 18.9 %collective-permute-start.17 = (s32[2]{0:T(128)S(1)}, s32[2]{0:T(128)S(1)}, u32[]{:S(2)}, u32[]{:S(2)}) collective-permute-start(s32[2]{0:T(128)S(1)} %slice_bitcast_fusion.4), channel_id=1, source_target_pairs={{0,4},{4,0},{8,12},{12,8},{1,5},{5,1},{9,13},{13,9},{2,6},{6,2},{1... | collective-permute-start | bytes 32 | tf_op jit(solution)/shard_map/ppermute | solution.py:248
  14.6 20.5 %collective-permute-start.16 = (f32[2,2,1536]{2,1,0:T(2,128)}, f32[2,2,1536]{2,1,0:T(2,128)}, u32[]{:S(2)}, u32[]{:S(2)}) collective-permute-start(f32[2,2,1536]{2,1,0:T(2,128)} %slice_bitcast_fusion.3), channel_id=1, source_target_pairs={{0,4},{4,0},{8,12},{12,8},{1,5},{5,1},{9,13},{13,9},{2,6},{6,2},{1... | collective-permute-start | bytes 73736 | tf_op jit(solution)/shard_map/ppermute | solution.py:248
  15.5 21.5 %collective-permute-start.10 = (f32[2,5,1536]{2,1,0:T(8,128)S(1)}, f32[2,5,1536]{2,1,0:T(8,128)}, u32[]{:S(2)}, u32[]{:S(2)}) collective-permute-start(f32[2,5,1536]{2,1,0:T(8,128)S(1)} %bitcast.108), channel_id=1, source_target_pairs={{0,4},{4,0},{8,12},{12,8},{1,5},{5,1},{9,13},{13,9},{2,6},{6,2},{1... | collective-permute-start | bytes 184328 | tf_op jit(solution)/shard_map/ppermute | solution.py:248
  17.8 20.8 %collective-permute-start.12 = (bf16[2,24,1536]{2,1,0:T(8,128)(2,1)}, bf16[2,24,1536]{2,1,0:T(8,128)(2,1)}, u32[]{:S(2)}, u32[]{:S(2)}) collective-permute-start(bf16[2,24,1536]{2,1,0:T(8,128)(2,1)} %get-tuple-element.37), channel_id=1, source_target_pairs={{0,4},{4,0},{8,12},{12,8},{1,5},{5,1},{9,13},{13,9},{2,6},{6,2},{1... | collective-permute-start | bytes 442376 | tf_op jit(solution)/shard_map/ppermute | solution.py:248
  18.6 24.9 %collective-permute-start.5 = (bf16[48,1536]{1,0:T(8,128)(2,1)}, bf16[48,1536]{1,0:T(8,128)(2,1)S(1)}, u32[]{:S(2)}, u32[]{:S(2)}) collective-permute-start(bf16[48,1536]{1,0:T(8,128)(2,1)} %get-tuple-element.29), channel_id=1, source_target_pairs={{0,3},{1,2},{2,1},{3,0},{4,7},{5,6},{6,5},{7,4},{8,11},{9,10},{10,... | collective-permute-start | bytes 442376 | tf_op jit(solution)/shard_map/ppermute | solution.py:251
  31.7 11.9 %collective-permute-start.4 = (bf16[48,1536]{1,0:T(8,128)(2,1)}, bf16[48,1536]{1,0:T(8,128)(2,1)S(1)}, u32[]{:S(2)}, u32[]{:S(2)}) collective-permute-start(bf16[48,1536]{1,0:T(8,128)(2,1)} %get-tuple-element.30), channel_id=1, source_target_pairs={{0,2},{1,3},{2,0},{3,1},{4,6},{5,7},{6,4},{7,5},{8,10},{9,11},{10,... | collective-permute-start | bytes 442376 | tf_op jit(solution)/shard_map/ppermute | solution.py:251
  35.1 9.0 %collective-permute-start.3 = (bf16[48,1536]{1,0:T(8,128)(2,1)S(1)}, bf16[48,1536]{1,0:T(8,128)(2,1)S(1)}, u32[]{:S(2)}, u32[]{:S(2)}) collective-permute-start(bf16[48,1536]{1,0:T(8,128)(2,1)S(1)} %copy-done.23), channel_id=1, source_target_pairs={{0,1},{1,0},{2,3},{3,2},{4,5},{5,4},{6,7},{7,6},{8,9},{9,8},{10,11... | collective-permute-start | bytes 442376 | tf_op jit(solution)/shard_map/ppermute | solution.py:251
  37.1 76.3 %collective-permute-start.6 = (bf16[2,128,1536]{2,1,0:T(8,128)(2,1)S(1)}, bf16[2,128,1536]{2,1,0:T(8,128)(2,1)S(1)}, u32[]{:S(2)}, u32[]{:S(2)}) collective-permute-start(bf16[2,128,1536]{2,1,0:T(8,128)(2,1)S(1)} %copy-done.14), channel_id=1, source_target_pairs={{0,4},{4,0},{8,12},{12,8},{1,5},{5,1},{9,13},{13,9},{2,6},{6,2},{1... | collective-permute-start | bytes 2359304 | tf_op jit(solution)/shard_map/ppermute | solution.py:248
  38.6 79.9 %collective-permute-start.2 = (bf16[256,1536]{1,0:T(8,128)(2,1)}, bf16[256,1536]{1,0:T(8,128)(2,1)S(1)}, u32[]{:S(2)}, u32[]{:S(2)}) collective-permute-start(bf16[256,1536]{1,0:T(8,128)(2,1)} %get-tuple-element.19), channel_id=1, source_target_pairs={{0,3},{1,2},{2,1},{3,0},{4,7},{5,6},{6,5},{7,4},{8,11},{9,10},{10,... | collective-permute-start | bytes 2359304 | tf_op jit(solution)/shard_map/ppermute | solution.py:251
  43.5 70.2 %copy-start.15 = (bf16[48,1536]{1,0:T(8,128)(2,1)}, bf16[48,1536]{1,0:T(8,128)(2,1)S(1)}, u32[]{:S(2)}) copy-start(bf16[48,1536]{1,0:T(8,128)(2,1)S(1)} %collective-permute-done.5) | copy-start | bytes 442372
  43.5 22.0 %collective-permute-start.15 = (bf16[24,1536]{1,0:T(8,128)(2,1)S(1)}, bf16[24,1536]{1,0:T(8,128)(2,1)S(1)}, u32[]{:S(2)}, u32[]{:S(2)}) collective-permute-start(bf16[24,1536]{1,0:T(8,128)(2,1)S(1)} %get-tuple-element.33), channel_id=1, source_target_pairs={{0,3},{1,2},{2,1},{3,0},{4,7},{5,6},{6,5},{7,4},{8,11},{9,10},{10,... | collective-permute-start | bytes 221192 | tf_op jit(solution)/shard_map/ppermute | solution.py:251
  43.6 70.1 %copy-start.17 = (bf16[48,1536]{1,0:T(8,128)(2,1)}, bf16[48,1536]{1,0:T(8,128)(2,1)S(1)}, u32[]{:S(2)}) copy-start(bf16[48,1536]{1,0:T(8,128)(2,1)S(1)} %collective-permute-done.4) | copy-start | bytes 442372
  43.6 57.6 %collective-permute-start.14 = (bf16[24,1536]{1,0:T(8,128)(2,1)S(1)}, bf16[24,1536]{1,0:T(8,128)(2,1)S(1)}, u32[]{:S(2)}, u32[]{:S(2)}) collective-permute-start(bf16[24,1536]{1,0:T(8,128)(2,1)S(1)} %get-tuple-element.34), channel_id=1, source_target_pairs={{0,2},{1,3},{2,0},{3,1},{4,6},{5,7},{6,4},{7,5},{8,10},{9,11},{10,... | collective-permute-start | bytes 221192 | tf_op jit(solution)/shard_map/ppermute | solution.py:251
  44.2 68.8 %collective-permute-start.13 = (bf16[24,1536]{1,0:T(8,128)(2,1)S(1)}, bf16[24,1536]{1,0:T(8,128)(2,1)S(1)}, u32[]{:S(2)}, u32[]{:S(2)}) collective-permute-start(bf16[24,1536]{1,0:T(8,128)(2,1)S(1)} %get-tuple-element.35), channel_id=1, source_target_pairs={{0,1},{1,0},{2,3},{3,2},{4,5},{5,4},{6,7},{7,6},{8,9},{9,8},{10,11... | collective-permute-start | bytes 221192 | tf_op jit(solution)/shard_map/ppermute | solution.py:251
  48.1 65.6 %copy-start.36 = (f32[192]{0:T(256)}, f32[192]{0:T(256)S(1)}, u32[]{:S(2)}) copy-start(f32[192]{0:T(256)S(1)} %broadcast_multiply_fusion.4) | copy-start | bytes 2308
  65.5 85.4 %collective-permute-start.1 = (bf16[256,1536]{1,0:T(8,128)(2,1)}, bf16[256,1536]{1,0:T(8,128)(2,1)S(1)}, u32[]{:S(2)}, u32[]{:S(2)}) collective-permute-start(bf16[256,1536]{1,0:T(8,128)(2,1)} %get-tuple-element.20), channel_id=1, source_target_pairs={{0,2},{1,3},{2,0},{3,1},{4,6},{5,7},{6,4},{7,5},{8,10},{9,11},{10,... | collective-permute-start | bytes 2359304 | tf_op jit(solution)/shard_map/ppermute | solution.py:251
  101.2 51.6 %collective-permute-start = (bf16[256,1536]{1,0:T(8,128)(2,1)}, bf16[256,1536]{1,0:T(8,128)(2,1)S(1)}, u32[]{:S(2)}, u32[]{:S(2)}) collective-permute-start(bf16[256,1536]{1,0:T(8,128)(2,1)} %get-tuple-element.21), channel_id=1, source_target_pairs={{0,1},{1,0},{2,3},{3,2},{4,5},{5,4},{6,7},{7,6},{8,9},{9,8},{10,11... | collective-permute-start | bytes 2359304 | tf_op jit(solution)/shard_map/ppermute | solution.py:251
  113.7 43.1 %collective-permute-start.9 = (bf16[128,1536]{1,0:T(8,128)(2,1)S(1)}, bf16[128,1536]{1,0:T(8,128)(2,1)S(1)}, u32[]{:S(2)}, u32[]{:S(2)}) collective-permute-start(bf16[128,1536]{1,0:T(8,128)(2,1)S(1)} %get-tuple-element.23), channel_id=1, source_target_pairs={{0,3},{1,2},{2,1},{3,0},{4,7},{5,6},{6,5},{7,4},{8,11},{9,10},{10,... | collective-permute-start | bytes 1179656 | tf_op jit(solution)/shard_map/ppermute | solution.py:251
  117.8 60.9 %collective-permute-start.8 = (bf16[128,1536]{1,0:T(8,128)(2,1)S(1)}, bf16[128,1536]{1,0:T(8,128)(2,1)S(1)}, u32[]{:S(2)}, u32[]{:S(2)}) collective-permute-start(bf16[128,1536]{1,0:T(8,128)(2,1)S(1)} %get-tuple-element.24), channel_id=1, source_target_pairs={{0,2},{1,3},{2,0},{3,1},{4,6},{5,7},{6,4},{7,5},{8,10},{9,11},{10,... | collective-permute-start | bytes 1179656 | tf_op jit(solution)/shard_map/ppermute | solution.py:251
  118.5 60.3 %collective-permute-start.7 = (bf16[128,1536]{1,0:T(8,128)(2,1)S(1)}, bf16[128,1536]{1,0:T(8,128)(2,1)S(1)}, u32[]{:S(2)}, u32[]{:S(2)}) collective-permute-start(bf16[128,1536]{1,0:T(8,128)(2,1)S(1)} %get-tuple-element.25), channel_id=1, source_target_pairs={{0,1},{1,0},{2,3},{3,2},{4,5},{5,4},{6,7},{7,6},{8,9},{9,8},{10,11... | collective-permute-start | bytes 1179656 | tf_op jit(solution)/shard_map/ppermute | solution.py:251
  211.4 157.7 %collective-permute-start.18 = (bf16[96,2048]{1,0:T(8,128)(2,1)S(1)}, bf16[96,2048]{1,0:T(8,128)(2,1)S(1)}, u32[]{:S(2)}, u32[]{:S(2)}) collective-permute-start(bf16[96,2048]{1,0:T(8,128)(2,1)S(1)} %convolution_convert_fusion.3.refs_5_.refs_6_), channel_id=1, source_target_pairs={{0,4},{4,0},{8,12},{12,8},{1,5},{5,1},{9,13},{13,9},{2,6},{6,2},{1... | collective-permute-start | bytes 1179656 | tf_op jit(solution)/shard_map/ppermute | solution.py:248
  301.3 67.8 %collective-permute-start.11 = (bf16[512,2048]{1,0:T(8,128)(2,1)}, bf16[512,2048]{1,0:T(8,128)(2,1)S(1)}, u32[]{:S(2)}, u32[]{:S(2)}) collective-permute-start(bf16[512,2048]{1,0:T(8,128)(2,1)} %slice.146), channel_id=1, source_target_pairs={{0,4},{4,0},{8,12},{12,8},{1,5},{5,1},{9,13},{13,9},{2,6},{6,2},{1... | collective-permute-start | bytes 6291464 | tf_op jit(solution)/shard_map/ppermute | solution.py:248
  315.1 47.1 %copy-start.1 = (bf16[32,32,1536]{2,1,0:T(8,128)(2,1)S(1)}, bf16[32,32,1536]{2,1,0:T(8,128)(2,1)}, u32[]{:S(2)}) copy-start(bf16[32,32,1536]{2,1,0:T(8,128)(2,1)} %slice.141) | copy-start | bytes 9437188
  315.1 47.1 %copy-start.30 = (f32[1536]{0:T(1024)S(1)}, f32[1536]{0:T(1024)}, u32[]{:S(2)}) copy-start(f32[1536]{0:T(1024)} %get-tuple-element.5) | copy-start | bytes 18436
  398.9 5.0 %collective-permute-start.19 = (bf16[4,384,32]{1,2,0:T(8,128)(2,1)S(1)}, bf16[4,384,32]{1,2,0:T(8,128)(2,1)S(1)}, u32[]{:S(2)}, u32[]{:S(2)}) collective-permute-start(bf16[4,384,32]{1,2,0:T(8,128)(2,1)S(1)} %fusion.53), channel_id=1, source_target_pairs={{0,16},{16,0},{1,17},{17,1},{2,18},{18,2},{3,19},{19,3},{4,20},{20... | collective-permute-start | bytes 294920 | tf_op jit(solution)/shard_map/ppermute | solution.py:22
  404.0 6.2 %collective-permute-start.22 = (f32[384,32]{0,1:T(8,128)S(1)}, f32[384,32]{0,1:T(8,128)S(1)}, u32[]{:S(2)}, u32[]{:S(2)}) collective-permute-start(f32[384,32]{0,1:T(8,128)S(1)} %get-tuple-element.43), channel_id=1, source_target_pairs={{0,3},{1,2},{2,1},{3,0},{4,7},{5,6},{6,5},{7,4},{8,11},{9,10},{10,... | collective-permute-start | bytes 147464 | tf_op jit(solution)/shard_map/ppermute | solution.py:251
  406.0 5.8 %collective-permute-start.21 = (f32[384,32]{0,1:T(8,128)S(1)}, f32[384,32]{0,1:T(8,128)S(1)}, u32[]{:S(2)}, u32[]{:S(2)}) collective-permute-start(f32[384,32]{0,1:T(8,128)S(1)} %get-tuple-element.44), channel_id=1, source_target_pairs={{0,2},{1,3},{2,0},{3,1},{4,6},{5,7},{6,4},{7,5},{8,10},{9,11},{10,... | collective-permute-start | bytes 147464 | tf_op jit(solution)/shard_map/ppermute | solution.py:251
  407.0 4.7 %collective-permute-start.20 = (f32[384,32]{0,1:T(8,128)S(1)}, f32[384,32]{0,1:T(8,128)S(1)}, u32[]{:S(2)}, u32[]{:S(2)}) collective-permute-start(f32[384,32]{0,1:T(8,128)S(1)} %get-tuple-element.45), channel_id=1, source_target_pairs={{0,1},{1,0},{2,3},{3,2},{4,5},{5,4},{6,7},{7,6},{8,9},{9,8},{10,11... | collective-permute-start | bytes 147464 | tf_op jit(solution)/shard_map/ppermute | solution.py:251
  411.8 1.3 collective-permute-start.23
  (42 other events, 366.2 us)
Sparse Core Ops, SparseCore 0:
  10.9 108.2 all-gather.9
  122.7 84.4 all-gather.7
  210.1 80.5 all-gather.5

commit v2 on v1

--- a/solution.py
+++ b/solution.py
@@ -151,20 +151,26 @@
     for _ in range(texts):
         pieces.append((refs[at], refs[at + 1], refs[at + 2]))
         at += 3
-    q = q_ref[...] * jnp.asarray(0.125, jnp.bfloat16)
-    lane = lax.broadcasted_iota(jnp.int32, q.shape, 1)
-    halves = []
-    for head in range(2):
+    rows = q_ref.shape[0]
+    sub = min(256, rows)
+    lane = lax.broadcasted_iota(jnp.int32, (sub, 128), 1)
+    units = [(start, head) for start in range(0, rows, sub) for head in range(2)]
+
+    def score(start, head):
+        q = q_ref[start : start + sub, :] * jnp.asarray(0.125, jnp.bfloat16)
         mine = (lane < HD) if head == 0 else (lane >= HD)
-        q_head = jnp.where(mine, q, jnp.zeros_like(q))
+        q = jnp.where(mine, q, jnp.zeros_like(q))
         scores = []
         for k_ref, _, bias_ref in pieces:
             s = lax.dot_general(
-                q_head, k_ref[...], (((1,), (1,)), ((), ())), preferred_element_type=jnp.float32
+                q, k_ref[...], (((1,), (1,)), ((), ())), preferred_element_type=jnp.float32
             )
             if bias_ref is not None:
                 s = s + bias_ref[0:1, :]
             scores.append(s)
+        return scores
+
+    def mix(scores):
         top = functools.reduce(jnp.maximum, [jnp.max(s, axis=1, keepdims=True) for s in scores])
         top = top * LOG2E
         total = None
@@ -175,13 +181,23 @@
             total = part if total is None else total + part
             part = jnp.dot(p.astype(jnp.bfloat16), v_ref[...], preferred_element_type=jnp.float32)
             mixed = part if mixed is None else mixed + part
-        halves.append(mixed / total)
-    o_ref[...] = jnp.where(lane < HD, halves[0], halves[1]).astype(jnp.bfloat16)
+        return mixed / total
+
+    halves = []
+    ahead = score(*units[0])
+    for index, (start, head) in enumerate(units):
+        scores = ahead
+        if index + 1 < len(units):
+            ahead = score(*units[index + 1])
+        halves.append(mix(scores))
+        if head == 1:
+            joined = jnp.where(lane < HD, halves[-2], halves[-1])
+            o_ref[start : start + sub, :] = joined.astype(jnp.bfloat16)
 
 
 def attend(query, width, images, texts):
     rows = query.shape[0]
-    block = min(256, rows)
+    block = min(512, rows)
     pairs = width // 128
     args = [query]
     specs = [pl.BlockSpec((block, 128), lambda h, i: (i, h))]
@@ -207,7 +223,7 @@
         in_specs=specs,
         out_specs=pl.BlockSpec((block, 128), lambda h, i: (i, h)),
         out_shape=jax.ShapeDtypeStruct((rows, width), jnp.bfloat16),
-        compiler_params=pltpu.CompilerParams(vmem_limit_bytes=28 * 2**20),
+        compiler_params=pltpu.CompilerParams(vmem_limit_bytes=32 * 2**20),
         cost_estimate=pl.CostEstimate(
             flops=16 * rows * keys * width,
             bytes_accessed=4 * (rows + keys) * width,
@@ -263,36 +279,59 @@
             jnp.concatenate([other, mine], axis),
         )
 
-    def halved(value, rows):
-        kept = lax.dynamic_slice_in_dim(value, core * rows, rows, 1)
-        sent = lax.dynamic_slice_in_dim(value, (1 - core) * rows, rows, 1)
-        return by_core(kept, swap(sent), 0)
+    length_row = jnp.broadcast_to(
+        text_lengths[0, ranks:].astype(jnp.float32)[:, None, None], (ranks // 2, 1, model_width)
+    )
+    facts = jnp.concatenate([img_mod[0, ranks:], txt_mod[0, ranks:], length_row], 1)
+    facts = pick(by_core(facts, swap(facts), 0), seq)
+    mods = img_mod.shape[2]
+    mod_pair, tmod_pair = facts[:mods], facts[mods:-1]
+    len_pair = facts[-1, 0].astype(jnp.int32)
+    mod_own, tmod_own, len_own = pick(img_mod[0], seq), pick(txt_mod[0], seq), pick(text_lengths[0], seq)
+
+    hidden = jnp.concatenate([img_hidden[0, :ranks], txt_hidden[0, :ranks]], 1)
+    own_rows = spread(hidden)
 
     full_img = lax.all_gather(w_img_qkv, ALL_AXES, axis=0, tiled=True)
-    full_txt = lax.all_gather(w_txt_qkv[:, attn_width:], ALL_AXES, axis=0, tiled=True)
+    txt_lines, full_img, own_rows = lax.optimization_barrier(
+        (w_txt_qkv[:, attn_width:], full_img, own_rows)
+    )
+    full_txt = lax.all_gather(txt_lines, ALL_AXES, axis=0, tiled=True)
+
+    kept = jnp.concatenate(
+        [
+            lax.dynamic_slice_in_dim(img_hidden[0, ranks:], core * img_half, img_half, 1),
+            lax.dynamic_slice_in_dim(txt_hidden[0, ranks:], core * txt_half, txt_half, 1),
+        ],
+        1,
+    )
+    given = jnp.concatenate(
+        [
+            lax.dynamic_slice_in_dim(img_hidden[0, ranks:], (1 - core) * img_half, img_half, 1),
+            lax.dynamic_slice_in_dim(txt_hidden[0, ranks:], (1 - core) * txt_half, txt_half, 1),
+        ],
+        1,
+    )
+    pair_rows = spread(by_core(kept, swap(given), 0))
+    img_own = jnp.concatenate([r[:img_rows] for r in own_rows], 0)
+    txt_own = jnp.concatenate([r[img_rows:] for r in own_rows], 0)
+    img_pair = jnp.concatenate([r[:img_half] for r in pair_rows], 0)
+    txt_pair = jnp.concatenate([r[img_half:] for r in pair_rows], 0)
+
+    def dot(left, right):
+        return jnp.dot(left, right, preferred_element_type=jnp.float32)
+
+    def places(start, count):
+        slots = jnp.arange(ranks, dtype=jnp.int32) ^ seq
+        return (slots[:, None] * txt_rows + start + jnp.arange(count, dtype=jnp.int32)[None]).reshape(-1)
+
+    qkv_own = dot(modulate(img_own, mod_own[0], mod_own[1]), full_img).astype(jnp.bfloat16)
     head_lines = w_head.size // model_width
     tail = jnp.concatenate([w_out, w_head.reshape(head_lines, model_width)], 0)
+    tail, full_txt, qkv_own = lax.optimization_barrier((tail, full_txt, qkv_own))
     full_tail = lax.all_gather(tail, ALL_AXES, axis=0, tiled=False)
     full_out = full_tail[:, : w_out.shape[0]].reshape(attn_width, model_width)
     full_head = full_tail[:, w_out.shape[0] :].reshape(model_width, w_head.shape[1])
-
-    img_own = jnp.concatenate(spread(img_hidden[0, :ranks]), 0)
-    txt_own = jnp.concatenate(spread(txt_hidden[0, :ranks]), 0)
-    img_pair = jnp.concatenate(spread(halved(img_hidden[0, ranks:], img_half)), 0)
-    txt_pair = jnp.concatenate(spread(halved(txt_hidden[0, ranks:], txt_half)), 0)
-    mod_own, tmod_own, len_own = pick(img_mod[0], seq), pick(txt_mod[0], seq), pick(text_lengths[0], seq)
-    mod_pair = pick(by_core(img_mod[0, ranks:], swap(img_mod[0, ranks:]), 0), seq)
-    tmod_pair = pick(by_core(txt_mod[0, ranks:], swap(txt_mod[0, ranks:]), 0), seq)
-    len_pair = pick(by_core(text_lengths[0, ranks:], swap(text_lengths[0, ranks:]), 0), seq)
-
-    def dot(left, right):
-        return jnp.dot(left, right, preferred_element_type=jnp.float32)
-
-    def places(start, count):
-        slots = jnp.arange(ranks, dtype=jnp.int32) ^ seq
-        return (slots[:, None] * txt_rows + start + jnp.arange(count, dtype=jnp.int32)[None]).reshape(-1)
-
-    qkv_own = dot(modulate(img_own, mod_own[0], mod_own[1]), full_img).astype(jnp.bfloat16)
     kvt_own = dot(modulate(txt_own, tmod_own[0], tmod_own[1]), full_txt).astype(jnp.bfloat16)
     qkv_pair = dot(modulate(img_pair, mod_pair[0], mod_pair[1]), full_img).astype(jnp.bfloat16)
     kvt_pair = dot(modulate(txt_pair, tmod_pair[0], tmod_pair[1]), full_txt).astype(jnp.bfloat16)

time: 421 us -> 354 us (0.84)
  starting transfers between devices: 68.6 us -> 16.8 us
  Pallas kernels: 73.1 us -> 52.5 us
  local copies, waits for them, and re-layouts: 23.4 us -> 29.7 us
  matrix products: 34.8 us -> 39.3 us
    ppermute x15 -> x9, waiting for transfers between devices: 80.3 us -> 170 us  [hop(): return lax.ppermute(value, 'seq', [(r, r ^ k) for r in range(ranks)])]
    all_gather x1, waiting for transfers between devices: 77.3 us -> 4.99 us  [moved(): full_img = lax.all_gather(w_img_qkv, ALL_AXES, axis=0, tiled=True)]
    ppermute x15 -> x9, starting transfers between devices: 65.3 us -> 13.6 us  [hop(): return lax.ppermute(value, 'seq', [(r, r ^ k) for r in range(ranks)])]
    pallas_call x2, Pallas kernels: 73.1 us -> 52.5 us  [attend(): pl.pallas_call(functools.partial(attend_kernel, len(images), len(texts)),...]
    all_gather x1, waiting for transfers between devices: 20.2 us -> 0.01 us  [moved(): full_txt = lax.all_gather(txt_lines, ALL_AXES, axis=0, tiled=True)]
    slice x4 -> x19, local copies, waits for them, and re-layouts: 0.01 us -> 14 us  [the longest x4 4.47 us: moved(): img_own = jnp.concatenate([r[:img_rows] for r in own_rows], 0)]
    dot_general x8, matrix products: 34.8 us -> 39.3 us  [dot(): return jnp.dot(left, right, preferred_element_type=jnp.float32)]
  transfers between devices with their start and end apart: 27 -> 18, of which waited for: 11 -> 11; matrix products, arithmetic and copies ran while one was open for 17% -> 19% of each run, Pallas kernels for 11% -> 15%
where the time goes in v2:
time: 354 us; the launch traced here: 353 us
  waiting for transfers between devices  181 us (51%)
  Pallas kernels  52.5 us (15%)
  matrix products  39.3 us (11%)
  local copies, waits for them, and re-layouts  29.7 us (8%)
  other arithmetic  18.5 us (5%)
  starting transfers between devices  16.8 us (5%)
  between operations  15.9 us (4%)
    ppermute x9, waiting for transfers between devices, hop(): return lax.ppermute(value, 'seq', [(r, r ^ k) for r in range(ranks)])  170 us
    pallas_call x2, Pallas kernels, attend(): pl.pallas_call(functools.partial(attend_kernel, len(images), len(texts)),...  52.5 us
    dot_general x8, matrix products, dot(): return jnp.dot(left, right, preferred_element_type=jnp.float32)  39.3 us
    ppermute x9, starting transfers between devices, hop(): return lax.ppermute(value, 'seq', [(r, r ^ k) for r in range(ranks)])  13.6 us
  transfers between devices with their start and end apart: 18, of which 11 were waited for; matrix products, arithmetic and copies ran while one was open for 19% of the time, Pallas kernels for 15%

profile of v2, /device:TPU:0, one launch (start us, length us, event | category | flops | bytes accessed | tf_op | source)
XLA Modules:
  0.0 353.3 jit_solution(14073874581058994863)
XLA Ops:
  9.1 2.1 slice_bitcast_fusion
  11.2 1.6 fusion.29
  12.8 5.0 %collective-permute-start.2 = (bf16[304,1536]{1,0:T(8,128)(2,1)}, bf16[304,1536]{1,0:T(8,128)(2,1)}, u32[]{:S(2)}, u32[]{:S(2)}) collective-permute-start(bf16[304,1536]{1,0:T(8,128)(2,1)} %get-tuple-element.36), channel_id=1, source_target_pairs={{0,3},{1,2},{2,1},{3,0},{4,7},{5,6},{6,5},{7,4},{8,11},{9,10},{10,... | collective-permute-start | bytes 2801672 | tf_op jit(solution)/shard_map/ppermute | solution.py:267
  19.2 24.0 %collective-permute-done.2 = bf16[304,1536]{1,0:T(8,128)(2,1)} collective-permute-done((bf16[304,1536]{1,0:T(8,128)(2,1)}, bf16[304,1536]{1,0:T(8,128)(2,1)}, u32[]{:S(2)}, u32[]{:S(2)}) %collective-permute-start.2) | collective-permute-done | bytes 933920 | tf_op jit(solution)/shard_map/ppermute | solution.py:267
  43.2 32.0 %collective-permute-done = bf16[304,1536]{1,0:T(8,128)(2,1)} collective-permute-done((bf16[304,1536]{1,0:T(8,128)(2,1)}, bf16[304,1536]{1,0:T(8,128)(2,1)}, u32[]{:S(2)}, u32[]{:S(2)}) %collective-permute-start) | collective-permute-done | bytes 933920 | tf_op jit(solution)/shard_map/ppermute | solution.py:267
  75.2 64.4 %collective-permute-done.1 = bf16[304,1536]{1,0:T(8,128)(2,1)} collective-permute-done((bf16[304,1536]{1,0:T(8,128)(2,1)}, bf16[304,1536]{1,0:T(8,128)(2,1)}, u32[]{:S(2)}, u32[]{:S(2)}) %collective-permute-start.1) | collective-permute-done | bytes 933920 | tf_op jit(solution)/shard_map/ppermute | solution.py:267
  139.6 5.0 %all-gather.6.cloned.1.call-done = bf16[1536,3072]{1,0:T(8,128)(2,1)} async-done(((bf16[48,3072]{1,0:T(8,128)(2,1)}), bf16[1536,3072]{1,0:T(8,128)(2,1)}) %all-gather.6.cloned.1.call-update) | async-done | bytes 9437200 | tf_op jit(solution)/shard_map/all_gather | solution.py:295
  150.7 1.7 broadcast_select_fusion
  154.7 2.2 maximum_select_fusion
  158.1 2.4 collective-permute-start.6
  162.5 11.9 %collective-permute-done.4 = bf16[152,1536]{1,0:T(8,128)(2,1)} collective-permute-done((bf16[152,1536]{1,0:T(8,128)(2,1)}, bf16[152,1536]{1,0:T(8,128)(2,1)}, u32[]{:S(2)}, u32[]{:S(2)}) %collective-permute-start.4) | collective-permute-done | bytes 466976 | tf_op jit(solution)/shard_map/ppermute | solution.py:267
  176.4 13.4 %collective-permute-done.6 = bf16[152,1536]{1,0:T(8,128)(2,1)} collective-permute-done((bf16[152,1536]{1,0:T(8,128)(2,1)}, bf16[152,1536]{1,0:T(8,128)(2,1)}, u32[]{:S(2)}, u32[]{:S(2)}) %collective-permute-start.6) | collective-permute-done | bytes 466976 | tf_op jit(solution)/shard_map/ppermute | solution.py:267
  191.7 22.4 %collective-permute-done.5 = bf16[152,1536]{1,0:T(8,128)(2,1)} collective-permute-done((bf16[152,1536]{1,0:T(8,128)(2,1)}, bf16[152,1536]{1,0:T(8,128)(2,1)}, u32[]{:S(2)}, u32[]{:S(2)}) %collective-permute-start.5) | collective-permute-done | bytes 466976 | tf_op jit(solution)/shard_map/ppermute | solution.py:267
  216.8 1.5 slice.181
  218.3 1.5 slice.182
  219.8 1.5 slice.183
  221.9 2.9 fusion.2
  224.9 18.6 %convolution_convert_fusion.refs_0_.refs_1_.refs_2_ = bf16[1024,3072]{1,0:T(8,128)(2,1)} fusion(bf16[1536,3072]{1,0:T(8,128)(2,1)} %all-gather.6.cloned.1.call-done, f32[1536]{0:T(1024)S(1)} %get-tuple-element.21, f32[1536]{0:T(1024)S(1)} %get-tuple-element.22, f32[1024]{0:T(1024)S(1)} %add_rsqrt_fusion.1, f32[1024]{0:T(1024)S(1)} %broadcast_multiply_fusion.1, ...), kind=kOutput, calls=%fused_computation.15 | convolution fusion | flops 9687269376 | bytes 18894848 | tf_op jit(solution)/shard_map/dot_general | solution.py:322
  247.4 10.7 %convolution_convert_fusion.1.refs_0_.refs_1_.refs_2_ = bf16[512,3072]{1,0:T(8,128)(2,1)S(1)} fusion(bf16[1536,3072]{1,0:T(8,128)(2,1)} %all-gather.6.cloned.1.call-done, f32[1536]{0:T(1024)S(1)} %get-tuple-element.30, f32[1536]{0:T(1024)S(1)} %get-tuple-element.31, f32[512]{0:T(512)S(1)} %add_rsqrt_fusion.3, f32[512]{0:T(512)S(1)} %broadcast_multiply_fusion.3, ...), kind=kOutput, calls=%fused_computation.19 | convolution fusion | flops 4843634688 | bytes 14172160 | tf_op jit(solution)/shard_map/dot_general | solution.py:322
  260.6 1.5 convolution_convert_fusion.2.refs_3_.refs_4_
  262.3 34.4 %shard_map.122 = bf16[1024,1024]{1,0:T(8,128)(2,1)S(1)} custom-call(bf16[1024,3072]{1,0:T(8,128)(2,1)S(1)} %bitcast.98, bf16[1024,3072]{1,0:T(8,128)(2,1)S(1)} %bitcast.98, bf16[1024,3072]{1,0:T(8,128)(2,1)S(1)} %bitcast.98, bf16[192,2048]{1,0:T(8,128)(2,1)S(1)} %convolution_convert_fusion.2.refs_3_.refs_4_, ...), custom_call_target="tpu_custom_call" | custom-call | flops 20401094656 | bytes 9175040 | tf_op jit(solution)/shard_map/pallas_call | solution.py:220
  296.8 18.1 %shard_map.123 = bf16[512,1024]{1,0:T(8,128)(2,1)S(1)} custom-call(bf16[512,3072]{1,0:T(8,128)(2,1)S(1)} %convolution_convert_fusion.1.refs_0_.refs_1_.refs_2_, bf16[512,3072]{1,0:T(8,128)(2,1)S(1)} %convolution_convert_fusion.1.refs_0_.refs_1_.refs_2_, bf16[512,3072]{1,0:T(8,128)(2,1)S(1)} %convolution_convert_fusion.1.refs_0_.refs_1_.refs_2_, ...), custom_call_target="tpu_custom_call" | custom-call | flops 10200547328 | bytes 7077888 | tf_op jit(solution)/shard_map/pallas_call | solution.py:220
  314.9 1.9 slice.228
  316.8 1.2 reshape.279
  318.1 2.3 slice.227
  320.9 3.6 %fusion.90 = (f32[1024]{0:T(1024)S(1)}, f32[1024,1536]{1,0:T(8,128)S(1)}) fusion(bf16[1024,1024]{1,0:T(8,128)(2,1)S(1)} %shard_map.122, bf16[1024,1536]{1,0:T(8,128)(2,1)S(1)} %bitcast.103, f32[1536]{0:T(1024)S(1)} %copy-done.25, bf16[256,1536]{1,0:T(8,128)(2,1)S(1)} %copy-done.7, bf16[256,1536]{1,0:T(8,128)(2,1)S(1)} %copy-done.5, ...), kind=kOutput, calls=%fused_computation.199 | convolution fusion | flops 3238525952 | bytes 14690304 | tf_op jit(solution)/shard_map/dot_general | solution.py:322
  325.9 1.9 fusion.91
  328.5 1.3 add_convert_fusion
  332.2 1.7 collective-permute-start.10
  333.9 3.2 collective-permute-done.10
  337.1 2.1 collective-permute-start.13
  339.4 2.2 collective-permute-start.11
  (186 shorter events, 36.8 us)
Async XLA Ops:
  7.2 137.4 %all-gather.6.cloned.1.call-start = ((), (), s32[]{:S(2)}) async-start(), calls=%async_computation | async-start | bytes 9732096 | tf_op jit(solution)/shard_map/all_gather | solution.py:295
  7.9 235.6 %all-gather.8.cloned.1.call-start = ((), (), s32[]{:S(2)}) async-start(), calls=%async_computation.1 | async-start | bytes 6488064 | tf_op jit(solution)/shard_map/all_gather | solution.py:299
  11.2 7.3 %copy-start.19 = (bf16[48,3072]{1,0:T(8,128)(2,1)S(1)}, bf16[48,3072]{1,0:T(8,128)(2,1)}, u32[]{:S(2)}) copy-start(bf16[48,3072]{1,0:T(8,128)(2,1)} %param.16) | copy-start | bytes 884740
  11.2 133.5 %slice-start.7 = ((f32[1,6,2,1536]{3,2,1,0:T(2,128)}), f32[1,2,2,1536]{3,2,1,0:T(2,128)S(1)}, s32[]{:S(2)}) async-start(f32[1,6,2,1536]{3,2,1,0:T(2,128)} %param.14), calls=%async_computation.10 | async-start | bytes 49152 | tf_op jit(solution)/shard_map/slice | solution.py:285
  11.2 133.5 %slice-start.6 = ((f32[1,6,5,1536]{3,0,2,1:T(1,128)}), f32[1,2,5,1536]{3,0,2,1:T(1,128)S(1)}, s32[]{:S(2)}) async-start(f32[1,6,5,1536]{3,0,2,1:T(1,128)} %param.13), calls=%async_computation.9 | async-start | bytes 122880 | tf_op jit(solution)/shard_map/slice | solution.py:285
  11.2 133.5 %copy-start.30 = (s32[1,6]{1,0:T(1,128)S(1)}, s32[1,6]{1,0:T(1,128)}, u32[]{:S(2)}) copy-start(s32[1,6]{1,0:T(1,128)} %param.19) | copy-start | bytes 76
  12.8 132.5 %slice-start.5 = ((bf16[1,6,48,1536]{3,2,1,0:T(8,128)(2,1)}), bf16[1,2,48,1536]{3,2,1,0:T(8,128)(2,1)S(1)}, s32[]{:S(2)}) async-start(bf16[1,6,48,1536]{3,2,1,0:T(8,128)(2,1)} %param.12), calls=%async_computation.8 | async-start | bytes 589824 | tf_op jit(solution)/shard_map/slice | solution.py:304
  12.8 132.5 %slice-start.4 = ((bf16[1,6,256,1536]{3,2,1,0:T(8,128)(2,1)}), bf16[1,2,256,1536]{3,2,1,0:T(8,128)(2,1)S(1)}, s32[]{:S(2)}) async-start(bf16[1,6,256,1536]{3,2,1,0:T(8,128)(2,1)} %param.11), calls=%async_computation.7 | async-start | bytes 3145728 | tf_op jit(solution)/shard_map/slice | solution.py:303
  12.8 30.4 %collective-permute-start.2 = (bf16[304,1536]{1,0:T(8,128)(2,1)}, bf16[304,1536]{1,0:T(8,128)(2,1)}, u32[]{:S(2)}, u32[]{:S(2)}) collective-permute-start(bf16[304,1536]{1,0:T(8,128)(2,1)} %get-tuple-element.36), channel_id=1, source_target_pairs={{0,3},{1,2},{2,1},{3,0},{4,7},{5,6},{6,5},{7,4},{8,11},{9,10},{10,... | collective-permute-start | bytes 2801672 | tf_op jit(solution)/shard_map/ppermute | solution.py:267
  17.9 57.3 %collective-permute-start = (bf16[304,1536]{1,0:T(8,128)(2,1)}, bf16[304,1536]{1,0:T(8,128)(2,1)}, u32[]{:S(2)}, u32[]{:S(2)}) collective-permute-start(bf16[304,1536]{1,0:T(8,128)(2,1)} %get-tuple-element.38), channel_id=1, source_target_pairs={{0,1},{1,0},{2,3},{3,2},{4,5},{5,4},{6,7},{7,6},{8,9},{9,8},{10,11... | collective-permute-start | bytes 2801672 | tf_op jit(solution)/shard_map/ppermute | solution.py:267
  17.9 121.7 %collective-permute-start.1 = (bf16[304,1536]{1,0:T(8,128)(2,1)}, bf16[304,1536]{1,0:T(8,128)(2,1)}, u32[]{:S(2)}, u32[]{:S(2)}) collective-permute-start(bf16[304,1536]{1,0:T(8,128)(2,1)} %get-tuple-element.39), channel_id=1, source_target_pairs={{0,2},{1,3},{2,0},{3,1},{4,6},{5,7},{6,4},{7,5},{8,10},{9,11},{10,... | collective-permute-start | bytes 2801672 | tf_op jit(solution)/shard_map/ppermute | solution.py:267
  144.6 170.3 %all-gather.10.cloned.1.call-start = ((), (), s32[]{:S(2)}) async-start(), calls=%async_computation.2 | async-start | bytes 4055040 | tf_op jit(solution)/shard_map/all_gather | solution.py:332
  145.0 5.8 %collective-permute-start.7 = (f32[2,8,1536]{2,0,1:T(2,128)S(1)}, f32[2,8,1536]{2,0,1:T(2,128)}, u32[]{:S(2)}, u32[]{:S(2)}) collective-permute-start(f32[2,8,1536]{2,0,1:T(2,128)S(1)} %pad_maximum_fusion.9), channel_id=1, source_target_pairs={{0,4},{4,0},{8,12},{12,8},{1,5},{5,1},{9,13},{13,9},{2,6},{6,2},{1... | collective-permute-start | bytes 294920 | tf_op jit(solution)/shard_map/ppermute | solution.py:264
  146.4 7.3 %collective-permute-start.3 = (bf16[2,152,1536]{2,1,0:T(8,128)(2,1)S(1)}, bf16[2,152,1536]{2,1,0:T(8,128)(2,1)S(1)}, u32[]{:S(2)}, u32[]{:S(2)}) collective-permute-start(bf16[2,152,1536]{2,1,0:T(8,128)(2,1)S(1)} %pad_maximum_fusion.2), channel_id=1, source_target_pairs={{0,4},{4,0},{8,12},{12,8},{1,5},{5,1},{9,13},{13,9},{2,6},{6,2},{1... | collective-permute-start | bytes 2801672 | tf_op jit(solution)/shard_map/ppermute | solution.py:264
  158.1 16.3 %collective-permute-start.4 = (bf16[152,1536]{1,0:T(8,128)(2,1)}, bf16[152,1536]{1,0:T(8,128)(2,1)}, u32[]{:S(2)}, u32[]{:S(2)}) collective-permute-start(bf16[152,1536]{1,0:T(8,128)(2,1)} %get-tuple-element.40), channel_id=1, source_target_pairs={{0,1},{1,0},{2,3},{3,2},{4,5},{5,4},{6,7},{7,6},{8,9},{9,8},{10,11... | collective-permute-start | bytes 1400840 | tf_op jit(solution)/shard_map/ppermute | solution.py:267
  158.1 31.7 %collective-permute-start.6 = (bf16[152,1536]{1,0:T(8,128)(2,1)}, bf16[152,1536]{1,0:T(8,128)(2,1)}, u32[]{:S(2)}, u32[]{:S(2)}) collective-permute-start(bf16[152,1536]{1,0:T(8,128)(2,1)} %get-tuple-element.41), channel_id=1, source_target_pairs={{0,3},{1,2},{2,1},{3,0},{4,7},{5,6},{6,5},{7,4},{8,11},{9,10},{10,... | collective-permute-start | bytes 1400840 | tf_op jit(solution)/shard_map/ppermute | solution.py:267
  160.6 53.6 %collective-permute-start.5 = (bf16[152,1536]{1,0:T(8,128)(2,1)}, bf16[152,1536]{1,0:T(8,128)(2,1)}, u32[]{:S(2)}, u32[]{:S(2)}) collective-permute-start(bf16[152,1536]{1,0:T(8,128)(2,1)} %get-tuple-element.42), channel_id=1, source_target_pairs={{0,2},{1,3},{2,0},{3,1},{4,6},{5,7},{6,4},{7,5},{8,10},{9,11},{10,... | collective-permute-start | bytes 1400840 | tf_op jit(solution)/shard_map/ppermute | solution.py:267
  162.5 84.8 %copy-start.14 = (bf16[128,1536]{1,0:T(8,128)(2,1)}, bf16[128,1536]{1,0:T(8,128)(2,1)S(1)}, u32[]{:S(2)}) copy-start(bf16[128,1536]{1,0:T(8,128)(2,1)S(1)} %dynamic-slice_bitcast_fusion.5) | copy-start | bytes 1179652
  176.3 71.0 %copy-start.8 = (bf16[128,1536]{1,0:T(8,128)(2,1)}, bf16[128,1536]{1,0:T(8,128)(2,1)S(1)}, u32[]{:S(2)}) copy-start(bf16[128,1536]{1,0:T(8,128)(2,1)S(1)} %slice.229) | copy-start | bytes 1179652
  191.7 55.6 %copy-start.10 = (bf16[128,1536]{1,0:T(8,128)(2,1)}, bf16[128,1536]{1,0:T(8,128)(2,1)S(1)}, u32[]{:S(2)}) copy-start(bf16[128,1536]{1,0:T(8,128)(2,1)S(1)} %slice.231) | copy-start | bytes 1179652
  216.1 31.3 %copy-start.12 = (bf16[128,1536]{1,0:T(8,128)(2,1)}, bf16[128,1536]{1,0:T(8,128)(2,1)S(1)}, u32[]{:S(2)}) copy-start(bf16[128,1536]{1,0:T(8,128)(2,1)S(1)} %slice.230) | copy-start | bytes 1179652
  216.8 8.0 %copy-start = (bf16[256,1536]{1,0:T(8,128)(2,1)}, bf16[256,1536]{1,0:T(8,128)(2,1)S(1)}, u32[]{:S(2)}) copy-start(bf16[256,1536]{1,0:T(8,128)(2,1)S(1)} %slice.180) | copy-start | bytes 2359300
  245.1 13.8 %slice-start.2 = ((s8[6291456]{0:T(1024)(128)(4,1)}), s8[4194304]{0:T(1024)(128)(4,1)S(1)}, s32[]{:S(2)}) async-start(s8[6291456]{0:T(1024)(128)(4,1)} %bitcast.100), calls=%async_computation.5 | async-start | bytes 8388608
  247.4 11.5 %slice-start.3 = ((s8[6291456]{0:T(1024)(128)(4,1)}), s8[2097152]{0:T(1024)(128)(4,1)S(1)}, s32[]{:S(2)}) async-start(s8[6291456]{0:T(1024)(128)(4,1)} %bitcast.100), calls=%async_computation.6 | async-start | bytes 4194304
  258.2 38.5 %collective-permute-start.8 = (bf16[512,2048]{1,0:T(8,128)(2,1)S(1)}, bf16[512,2048]{1,0:T(8,128)(2,1)S(1)}, u32[]{:S(2)}, u32[]{:S(2)}) collective-permute-start(bf16[512,2048]{1,0:T(8,128)(2,1)S(1)} %slice.235), channel_id=1, source_target_pairs={{0,4},{4,0},{8,12},{12,8},{1,5},{5,1},{9,13},{13,9},{2,6},{6,2},{1... | collective-permute-start | bytes 6291464 | tf_op jit(solution)/shard_map/ppermute | solution.py:264
  260.1 36.7 %collective-permute-start.9 = (bf16[96,2048]{1,0:T(8,128)(2,1)S(1)}, bf16[96,2048]{1,0:T(8,128)(2,1)S(1)}, u32[]{:S(2)}, u32[]{:S(2)}) collective-permute-start(bf16[96,2048]{1,0:T(8,128)(2,1)S(1)} %convolution_convert_fusion.3.refs_5_.refs_6_), channel_id=1, source_target_pairs={{0,4},{4,0},{8,12},{12,8},{1,5},{5,1},{9,13},{13,9},{2,6},{6,2},{1... | collective-permute-start | bytes 1179656 | tf_op jit(solution)/shard_map/ppermute | solution.py:264
  331.5 14.5 %copy-start.18 = (f32[6,256,32]{1,2,0:T(8,128)S(1)}, f32[6,256,32]{1,2,0:T(8,128)}, u32[]{:S(2)}) copy-start(f32[6,256,32]{1,2,0:T(8,128)} %param.20) | copy-start | bytes 589828
  332.2 4.9 %collective-permute-start.10 = (bf16[4,384,32]{1,2,0:T(8,128)(2,1)S(1)}, bf16[4,384,32]{1,2,0:T(8,128)(2,1)S(1)}, u32[]{:S(2)}, u32[]{:S(2)}) collective-permute-start(bf16[4,384,32]{1,2,0:T(8,128)(2,1)S(1)} %fusion.61), channel_id=1, source_target_pairs={{0,16},{16,0},{1,17},{17,1},{2,18},{18,2},{3,19},{19,3},{4,20},{20... | collective-permute-start | bytes 294920 | tf_op jit(solution)/shard_map/ppermute | solution.py:22
  337.1 6.2 %collective-permute-start.13 = (f32[384,32]{0,1:T(8,128)S(1)}, f32[384,32]{0,1:T(8,128)S(1)}, u32[]{:S(2)}, u32[]{:S(2)}) collective-permute-start(f32[384,32]{0,1:T(8,128)S(1)} %get-tuple-element.52), channel_id=1, source_target_pairs={{0,3},{1,2},{2,1},{3,0},{4,7},{5,6},{6,5},{7,4},{8,11},{9,10},{10,... | collective-permute-start | bytes 147464 | tf_op jit(solution)/shard_map/ppermute | solution.py:267
  339.2 5.4 %collective-permute-start.12 = (f32[384,32]{0,1:T(8,128)S(1)}, f32[384,32]{0,1:T(8,128)S(1)}, u32[]{:S(2)}, u32[]{:S(2)}) collective-permute-start(f32[384,32]{0,1:T(8,128)S(1)} %get-tuple-element.53), channel_id=1, source_target_pairs={{0,2},{1,3},{2,0},{3,1},{4,6},{5,7},{6,4},{7,5},{8,10},{9,11},{10,... | collective-permute-start | bytes 147464 | tf_op jit(solution)/shard_map/ppermute | solution.py:267
  339.4 5.2 %collective-permute-start.11 = (f32[384,32]{0,1:T(8,128)S(1)}, f32[384,32]{0,1:T(8,128)S(1)}, u32[]{:S(2)}, u32[]{:S(2)}) collective-permute-start(f32[384,32]{0,1:T(8,128)S(1)} %get-tuple-element.54), channel_id=1, source_target_pairs={{0,1},{1,0},{2,3},{3,2},{4,5},{5,4},{6,7},{7,6},{8,9},{9,8},{10,11... | collective-permute-start | bytes 147464 | tf_op jit(solution)/shard_map/ppermute | solution.py:267
  344.7 1.3 collective-permute-start.14
  (25 other events, 62.0 us)
Sparse Core Ops, SparseCore 0:
  10.9 133.6 all-gather.5
  148.0 94.4 all-gather.7
  246.0 59.6 all-gather.9
